TPU v7x, 32 devices: a whole 2x2x4 slice. The times are simulated.
32 devices in a mesh: dp: 8 (over y, x, core), tensor: 4 (over z).
Axes of the slice: x: 2, y: 2, z: 4, core: 2. Of those that a mesh axis runs over, the one named last changes fastest.
Arguments:
- block_in: bfloat16 [8, 1024, 1024], P('dp', 'tensor'), may hold values from -6 to 6
- segment_ids: int32 [8, 1024], P('dp', 'tensor'), may hold values from 0 to 2, as said below
- norm1_gain: float32 [1024], replicated, may hold values from 0.1 to 1.9
- w_qkv: bfloat16 [3, 1024, 1024], P(None, 'dp', 'tensor'), may hold values from -0.1875 to 0.1875
- w_out: bfloat16 [1024, 1024], P('tensor', 'dp'), may hold values from -3 to 3
- norm2_gain: float32 [1024], replicated, may hold values from 0.1 to 1.9
- w_in: bfloat16 [2, 1024, 2624], P(None, 'dp', 'tensor'), may hold values from -0.1875 to 0.1875
- w_mlp_out: bfloat16 [2624, 1024], P('tensor', 'dp'), may hold values from -0.125 to 0.125
- out_grad: bfloat16 [8, 1024, 1024], P('dp', 'tensor'), may hold values from -6 to 6
Outputs:
- block_out: bfloat16 [8, 1024, 1024], P('dp', 'tensor')
- in_grad: float32 [8, 1024, 1024], P('dp', 'tensor')
- norm1_grad: float32 [1024], replicated
- w_qkv_grad: float32 [3, 1024, 1024], P(None, 'dp', 'tensor')
- w_out_grad: float32 [1024, 1024], P('tensor', 'dp')
- norm2_grad: float32 [1024], replicated
- w_in_grad: float32 [2, 1024, 2624], P(None, 'dp', 'tensor')
- w_mlp_out_grad: float32 [2624, 1024], P('tensor', 'dp')
Inputs may be any that keep to these rules, and one draw needn't show every extreme that they name: `segment_ids`: ids never fall along a sequence; each sequence holds three documents, the first starting at position 0 and the last ending at position 1023, both shorter than 256 tokens.
All inputs are finite; a program needn't handle non-finite values.
Results may differ from a plain program's by a relative error of at most 0.017.
Values may be sent and summed in bfloat16 or wider, within the bound.
No kernel may reach another device: no remote copies, remote signals or barrier semaphores. Data moves between devices by JAX's collectives and lax.ppermute only.
A program may use at most 128 MiB of HBM per device.

v0:
```python
import jax
import jax.numpy as jnp
from jax import lax
from jax.sharding import PartitionSpec as P

HEAD_DIM = 64


EPSILON = 1e-05
ROPE_BASE = 160000.0
MASKED = -1e30


def normalize(inputs):
    average = jnp.mean(inputs, axis=-1, keepdims=True)
    centred = inputs - average
    inv_std = lax.rsqrt(jnp.mean(centred * centred, axis=-1, keepdims=True) + EPSILON)
    return (centred * inv_std, inv_std)


def norm_back(grad_rows, gain, scaled, inv_std):
    grad_scaled = grad_rows * gain
    mean_grad = jnp.mean(grad_scaled, axis=-1, keepdims=True)
    mean_proj = jnp.mean(grad_scaled * scaled, axis=-1, keepdims=True)
    return (
        inv_std * (grad_scaled - mean_grad - scaled * mean_proj),
        jnp.sum(grad_rows * scaled, axis=0),
    )


def positions_of(segments):
    places = jnp.arange(segments.shape[0], dtype=jnp.int32)
    starts = jnp.concatenate([jnp.ones((1,), jnp.bool_), segments[1:] != segments[:-1]])
    first = lax.cummax(jnp.where(starts, places, jnp.zeros_like(places)), axis=0)
    return places - first


def rotary_tables(segments):
    half_dim = HEAD_DIM // 2
    freqs = jnp.power(ROPE_BASE, -jnp.arange(half_dim, dtype=jnp.float32) * 2.0 / HEAD_DIM)
    angles = positions_of(segments).astype(jnp.float32)[:, None] * freqs[None, :]
    return (jnp.cos(angles)[:, None, :], jnp.sin(angles)[:, None, :])


def rotate(inputs, cosine, sine):
    half_dim = inputs.shape[-1] // 2
    first, second = (inputs[..., :half_dim], inputs[..., half_dim:])
    return jnp.concatenate(
        [first * cosine - second * sine, second * cosine + first * sine], axis=-1
    )


def unrotate(grads, cosine, sine):
    half_dim = grads.shape[-1] // 2
    first, second = (grads[..., :half_dim], grads[..., half_dim:])
    return jnp.concatenate(
        [first * cosine + second * sine, second * cosine - first * sine], axis=-1
    )


def block_scores(query_block, key_rows, seg_block, segments, scale):
    raw = (
        jnp.einsum("qhd,khd->hqk", query_block, key_rows, preferred_element_type=jnp.float32)
        * scale
    )
    same = (seg_block[:, None] == segments[None, :])[None]
    return jnp.where(same, raw, MASKED)


def gated(act_in, gate_in):
    return jax.nn.gelu(act_in, approximate=False) * gate_in


def on_device(
    block_in, segment_ids, norm1_gain, w_qkv, w_out, norm2_gain, w_in, w_mlp_out, out_grad
):
    qkv_full, out_full = (
        lax.all_gather(w_qkv, "dp", axis=1, tiled=True),
        lax.all_gather(w_out, "dp", axis=1, tiled=True),
    )
    segments = lax.all_gather(segment_ids, "tensor", axis=1, tiled=True)[0]
    length = segments.shape[0]
    local_width = qkv_full.shape[2]
    heads = local_width // HEAD_DIM
    scale = HEAD_DIM ** (-0.5)
    block_rows = min(512, length)
    block_count = length // block_rows
    cosine, sine = rotary_tables(segments)
    x_piece = block_in[0].astype(jnp.float32)
    scaled1, inv_std1 = normalize(x_piece)
    normed = lax.all_gather(
        (scaled1 * norm1_gain).astype(jnp.bfloat16), "tensor", axis=0, tiled=True
    )
    projected = jnp.einsum("ld,cde->cle", normed, qkv_full, preferred_element_type=jnp.float32)
    query_rows = rotate(projected[0].reshape(length, heads, HEAD_DIM), cosine, sine).astype(
        jnp.bfloat16
    )
    key_rows = rotate(projected[1].reshape(length, heads, HEAD_DIM), cosine, sine).astype(
        jnp.bfloat16
    )
    value_rows = projected[2].astype(jnp.bfloat16).reshape(length, heads, HEAD_DIM)
    contexts = []
    log_totals = []
    for block_no in range(block_count):
        rows_here = slice(block_no * block_rows, (block_no + 1) * block_rows)
        scores = block_scores(query_rows[rows_here], key_rows, segments[rows_here], segments, scale)
        highest = jnp.max(scores, axis=-1, keepdims=True)
        weights = jnp.exp(scores - highest)
        totals = jnp.sum(weights, axis=-1, keepdims=True)
        log_totals.append(highest + jnp.log(totals))
        chances = (weights / totals).astype(jnp.bfloat16)
        contexts.append(
            jnp.einsum("hqk,khd->qhd", chances, value_rows, preferred_element_type=jnp.float32)
        )
    context = jnp.concatenate(contexts, axis=0).reshape(length, local_width).astype(jnp.bfloat16)
    own_context = lax.all_to_all(context, "tensor", split_axis=0, concat_axis=1, tiled=True)
    whole_out = lax.all_gather(out_full, "tensor", axis=0, tiled=True)
    branch = jnp.dot(own_context, whole_out, preferred_element_type=jnp.float32)
    hidden = x_piece + branch
    in_full, down_full = (
        lax.all_gather(w_in, "dp", axis=1, tiled=True),
        lax.all_gather(w_mlp_out, "dp", axis=1, tiled=True),
    )
    scaled2, inv_std2 = normalize(hidden)
    normed2, grad_out = (
        lax.all_gather((scaled2 * norm2_gain).astype(jnp.bfloat16), "tensor", axis=0, tiled=True),
        lax.all_gather(out_grad[0], "tensor", axis=0, tiled=True),
    )
    expanded = jnp.einsum("ld,cdf->clf", normed2, in_full, preferred_element_type=jnp.float32)
    product = gated(expanded[0], expanded[1]).astype(jnp.bfloat16)
    mlp_branch = lax.psum_scatter(
        jnp.dot(product, down_full, preferred_element_type=jnp.float32).astype(jnp.bfloat16),
        "tensor",
        scatter_dimension=0,
        tiled=True,
    ).astype(jnp.float32)
    block_out = (hidden + mlp_branch).astype(jnp.bfloat16)
    qkv_full, out_full, in_full, down_full = (
        lax.all_gather(w_qkv, "dp", axis=1, tiled=True),
        lax.all_gather(w_out, "dp", axis=1, tiled=True),
        lax.all_gather(w_in, "dp", axis=1, tiled=True),
        lax.all_gather(w_mlp_out, "dp", axis=1, tiled=True),
    )
    grad_product = jnp.einsum("ld,fd->lf", grad_out, down_full, preferred_element_type=jnp.float32)
    gate_value, gate_pull = jax.vjp(gated, expanded[0], expanded[1])
    grad_act, grad_gate = gate_pull(grad_product)
    grad_expanded = jnp.stack([grad_act, grad_gate]).astype(jnp.bfloat16)
    in_grad_local = jnp.einsum(
        "ld,clf->cdf", normed2, grad_expanded, preferred_element_type=jnp.float32
    )
    down_grad_local = jnp.einsum("lf,ld->fd", product, grad_out, preferred_element_type=jnp.float32)
    in_grad_part, down_grad_part = (
        lax.psum_scatter(
            in_grad_local.astype(jnp.bfloat16), "dp", scatter_dimension=1, tiled=True
        ).astype(jnp.float32),
        lax.psum_scatter(
            down_grad_local.astype(jnp.bfloat16), "dp", scatter_dimension=1, tiled=True
        ).astype(jnp.float32),
    )
    grad_normed2 = lax.psum_scatter(
        jnp.einsum("clf,cdf->ld", grad_expanded, in_full, preferred_element_type=jnp.float32),
        "tensor",
        scatter_dimension=0,
        tiled=True,
    )
    grad_hidden_norm, gain2_term = norm_back(grad_normed2, norm2_gain, scaled2, inv_std2)
    grad_hidden = out_grad[0].astype(jnp.float32) + grad_hidden_norm
    grad_rows = lax.all_gather(grad_hidden.astype(jnp.bfloat16), "tensor", axis=0, tiled=True)
    grad_context = jnp.einsum("ld,ed->le", grad_rows, out_full, preferred_element_type=jnp.float32)
    grad_context = grad_context.astype(jnp.bfloat16).reshape(length, heads, HEAD_DIM)
    out_grad_local = jnp.einsum("le,ld->ed", context, grad_rows, preferred_element_type=jnp.float32)
    grad_keys = jnp.zeros((length, heads, HEAD_DIM), jnp.float32)
    grad_values = jnp.zeros((length, heads, HEAD_DIM), jnp.float32)
    grad_queries = []
    for block_no in range(block_count):
        rows_here = slice(block_no * block_rows, (block_no + 1) * block_rows)
        scores = block_scores(query_rows[rows_here], key_rows, segments[rows_here], segments, scale)
        chances = jnp.exp(scores - log_totals[block_no])
        grad_chances = jnp.einsum(
            "qhd,khd->hqk", grad_context[rows_here], value_rows, preferred_element_type=jnp.float32
        )
        inner = jnp.sum(chances * grad_chances, axis=-1, keepdims=True)
        grad_scores = (chances * (grad_chances - inner)).astype(jnp.bfloat16)
        grad_queries.append(
            jnp.einsum("hqk,khd->qhd", grad_scores, key_rows, preferred_element_type=jnp.float32)
            * scale
        )
        grad_keys = (
            grad_keys
            + jnp.einsum(
                "hqk,qhd->khd",
                grad_scores,
                query_rows[rows_here],
                preferred_element_type=jnp.float32,
            )
            * scale
        )
        grad_values = grad_values + jnp.einsum(
            "hqk,qhd->khd",
            chances.astype(jnp.bfloat16),
            grad_context[rows_here],
            preferred_element_type=jnp.float32,
        )
    grad_query_all = unrotate(jnp.concatenate(grad_queries, axis=0), cosine, sine)
    grad_key_all = unrotate(grad_keys, cosine, sine)
    grad_projected = (
        jnp.stack([grad_query_all, grad_key_all, grad_values])
        .reshape(3, length, local_width)
        .astype(jnp.bfloat16)
    )
    qkv_grad_local = jnp.einsum(
        "ld,cle->cde", normed, grad_projected, preferred_element_type=jnp.float32
    )
    grad_normed1 = lax.psum_scatter(
        jnp.einsum(
            "cle,cde->ld", grad_projected, qkv_full, preferred_element_type=jnp.float32
        ).astype(jnp.bfloat16),
        "tensor",
        scatter_dimension=0,
        tiled=True,
    ).astype(jnp.float32)
    qkv_grad, out_grad_part = (
        lax.psum_scatter(
            qkv_grad_local.astype(jnp.bfloat16), "dp", scatter_dimension=1, tiled=True
        ).astype(jnp.float32),
        lax.psum_scatter(
            out_grad_local.astype(jnp.bfloat16), "dp", scatter_dimension=1, tiled=True
        ).astype(jnp.float32),
    )
    grad_input_norm, gain1_term = norm_back(grad_normed1, norm1_gain, scaled1, inv_std1)
    input_grad = grad_hidden + grad_input_norm
    gain1_grad, gain2_grad = lax.psum((gain1_term, gain2_term), ("dp", "tensor"))
    return (
        block_out[None],
        input_grad[None],
        gain1_grad,
        qkv_grad,
        out_grad_part,
        gain2_grad,
        in_grad_part,
        down_grad_part,
    )


def solution(mesh):
    in_specs = (
        P("dp", "tensor", None),
        P("dp", "tensor"),
        P(),
        P(None, "dp", "tensor"),
        P("tensor", "dp"),
        P(),
        P(None, "dp", "tensor"),
        P("tensor", "dp"),
        P("dp", "tensor", None),
    )
    out_specs = (
        P("dp", "tensor", None),
        P("dp", "tensor", None),
        P(),
        P(None, "dp", "tensor"),
        P("tensor", "dp"),
        P(),
        P(None, "dp", "tensor"),
        P("tensor", "dp"),
    )
    return jax.shard_map(
        on_device, mesh=mesh, in_specs=in_specs, out_specs=out_specs, check_vma=False
    )
```

profile of v0, /device:TPU:0, one launch (start us, length us, event | category | flops | bytes accessed | tf_op | source)
XLA Modules:
  0.0 753.7 jit_solution(4770385980877634397)
XLA Ops:
  13.8 13.6 %all_gather.40 = bf16[256,1024]{1,0:T(8,128)(2,1)} all-gather(bf16[256,128]{1,0:T(8,128)(2,1)S(1)} %copy-done.24), channel_id=1, replica_groups=mesh['dp'=8,'tensor'=4] {'dp'}, dimensions={1}, use_global_device_ids=true | all-gather | bytes 589824 | tf_op jit(solution)/shard_map/all_gather | solution.py:79
  29.2 11.2 %all_gather.38 = s32[1,1024]{1,0:T(1,128)S(1)} all-gather(s32[1,256]{1,0:T(1,128)S(1)} %copy-done.40), channel_id=1, replica_groups=mesh['dp'=8,'tensor'=4] {'tensor'}, dimensions={1}, use_global_device_ids=true | all-gather | bytes 5120 | tf_op jit(solution)/shard_map/all_gather | solution.py:81
  42.4 45.6 %all-gather.10.cloned.1.call-done = bf16[1024,1024]{1,0:T(8,128)(2,1)} async-done(((bf16[256,1024]{1,0:T(8,128)(2,1)}), bf16[1024,1024]{1,0:T(8,128)(2,1)}) %all-gather.10.cloned.1.call-update) | async-done | bytes 2097168 | tf_op jit(solution)/shard_map/all_gather | solution.py:91
  88.0 3.9 fusion.42
  109.1 36.3 %all-gather.14.cloned.1.call-done = bf16[1024,1024]{1,0:T(8,128)(2,1)} async-done(((bf16[256,1024]{1,0:T(8,128)(2,1)}), bf16[1024,1024]{1,0:T(8,128)(2,1)}) %all-gather.14.cloned.1.call-update) | async-done | bytes 2097168 | tf_op jit(solution)/shard_map/all_gather | solution.py:117
  149.4 21.3 %all-gather.20.cloned.1.call-done = bf16[656,1024]{1,0:T(8,128)(2,1)} async-done(((bf16[656,128]{1,0:T(8,128)(2,1)}), bf16[656,1024]{1,0:T(8,128)(2,1)}) %all-gather.20.cloned.1.call-update) | async-done | bytes 1343504 | tf_op jit(solution)/shard_map/all_gather | solution.py:122
  170.7 47.4 %all-gather.24.cloned.1.call-done = bf16[1,1024,1024]{2,1,0:T(8,128)(2,1)} async-done(((bf16[1,256,1024]{2,1,0:T(8,128)(2,1)}), bf16[1,1024,1024]{2,1,0:T(8,128)(2,1)}) %all-gather.24.cloned.1.call-update) | async-done | bytes 2097168 | tf_op jit(solution)/shard_map/all_gather | solution.py:127
  218.1 5.1 fusion.34
  223.2 26.2 %all-gather.18.cloned.1.call-done = bf16[2,1024,656]{1,2,0:T(8,128)(2,1)} async-done(((bf16[2,128,656]{1,2,0:T(8,128)(2,1)}), bf16[2,1024,656]{1,2,0:T(8,128)(2,1)}) %all-gather.18.cloned.1.call-update) | async-done | bytes 2686992 | tf_op jit(solution)/shard_map/all_gather | solution.py:121
  249.4 48.1 %all-gather.16.cloned.1.call-done = bf16[1024,1024]{1,0:T(8,128)(2,1)} async-done(((bf16[256,1024]{1,0:T(8,128)(2,1)}), bf16[1024,1024]{1,0:T(8,128)(2,1)}) %all-gather.16.cloned.1.call-update) | async-done | bytes 2097168 | tf_op jit(solution)/shard_map/all_gather | solution.py:126
  297.5 5.5 convolution_bitcast_fusion
  303.0 6.5 fusion.57
  313.2 5.0 convolution_bitcast_fusion.1
  318.2 5.0 convolution_convert_fusion
  323.3 70.6 %reduce-scatter.18.cloned.1.call-done = f32[256,1024]{1,0:T(8,128)} async-done(((f32[1024,1024]{1,0:T(8,128)}), f32[256,1024]{1,0:T(8,128)}) %reduce-scatter.18.cloned.1.call-update) | async-done | bytes 1048592 | tf_op jit(solution)/shard_map/reduce_scatter | solution.py:160
  396.8 43.9 %reduce-scatter.16.cloned.1.call-done = bf16[256,1024]{1,0:T(8,128)(2,1)} async-done(((bf16[1024,1024]{1,0:T(8,128)(2,1)}), bf16[256,1024]{1,0:T(8,128)(2,1)}) %reduce-scatter.16.cloned.1.call-update) | async-done | bytes 524304 | tf_op jit(solution)/shard_map/reduce_scatter | solution.py:131
  443.7 10.9 %reduce-scatter.28.cloned.1.call-start = ((), (), s32[]{:S(2)}) async-start(), calls=%async_computation.22 | async-start | bytes 1769472
  454.6 4.7 fusion.48
  462.0 6.9 convert_bitcast_fusion
  468.9 8.7 %copy.46 = bf16[2,1024,656]{2,0,1:T(2,128)(2,1)} copy(bf16[2,1024,656]{1,2,0:T(8,128)(2,1)} %convert_bitcast_fusion) | data formatting | bytes 5373952
  477.6 7.5 reshape.269
  485.2 3.9 all-gather.22.cloned.1.call-done
  491.5 5.5 multiply_reduce_fusion.1
  502.5 4.4 fusion.72
  506.9 5.4 multiply_reduce_fusion
  528.0 4.6 fusion.51
  537.3 5.1 bitcast_convert_fusion
  544.4 33.5 %reduce-scatter.26.cloned.1.call-done = bf16[128,1312]{1,0:T(8,128)(2,1)} async-done(((bf16[1024,1312]{1,0:T(8,128)(2,1)}), bf16[128,1312]{1,0:T(8,128)(2,1)}) %reduce-scatter.26.cloned.1.call-update) | async-done | bytes 335888
  580.8 34.6 %reduce-scatter.24.cloned.1.call-done = bf16[128,256]{1,0:T(8,128)(2,1)} async-done(((bf16[1024,256]{1,0:T(8,128)(2,1)}), bf16[128,256]{1,0:T(8,128)(2,1)}) %reduce-scatter.24.cloned.1.call-update) | async-done | bytes 65552
  617.0 40.0 %reduce-scatter.22.cloned.1.call-done = bf16[128,768]{1,0:T(8,128)(2,1)} async-done(((bf16[1024,768]{1,0:T(8,128)(2,1)}), bf16[128,768]{1,0:T(8,128)(2,1)}) %reduce-scatter.22.cloned.1.call-update) | async-done | bytes 196624
  659.2 43.9 %reduce-scatter.20.cloned.1.call-done = bf16[256,1024]{1,0:T(8,128)(2,1)} async-done(((bf16[1024,1024]{1,0:T(8,128)(2,1)}), bf16[256,1024]{1,0:T(8,128)(2,1)}) %reduce-scatter.20.cloned.1.call-update) | async-done | bytes 524304 | tf_op jit(solution)/shard_map/reduce_scatter | solution.py:214
  704.7 39.7 %all-reduce = (f32[1024]{0:T(1024)}, f32[1024]{0:T(1024)}) all-reduce(f32[1024]{0:T(1024)S(1)} %get-tuple-element.35, f32[1024]{0:T(1024)S(1)} %copy-done.37), channel_id=1, replica_groups=mesh['dp'=8,'tensor'=4] {'dp','tensor'}, use_global_device_ids=true, to_apply=%region_20.21 | all-reduce | flops 2048 | bytes 16384 | tf_op jit(solution)/shard_map/psum | solution.py:232
  (208 shorter events, 84.2 us)
Async XLA Ops:
  7.2 6.7 copy-start.24
  7.2 22.0 %copy-start.40 = (s32[1,256]{1,0:T(1,128)S(1)}, s32[1,256]{1,0:T(1,128)}, u32[]{:S(2)}) copy-start(s32[1,256]{1,0:T(1,128)} %param.10) | copy-start | bytes 3076
  7.2 35.2 %all-gather.12.cloned.1.call-start = ((), (), s32[]{:S(2)}) async-start(), calls=%async_computation.9 | async-start | bytes 1769472 | tf_op jit(solution)/shard_map/all_gather | solution.py:78
  9.0 79.0 %all-gather.10.cloned.1.call-start = ((), (), s32[]{:S(2)}) async-start(), calls=%async_computation.8 | async-start | bytes 2621440 | tf_op jit(solution)/shard_map/all_gather | solution.py:91
  10.2 32.1 %copy-start.35 = (f32[256]{0:T(256)}, f32[256]{0:T(256)S(1)}, u32[]{:S(2)}) copy-start(f32[256]{0:T(256)S(1)} %broadcast_multiply_fusion.5) | copy-start | bytes 3076
  11.6 80.3 %copy-start.38 = (f32[256]{0:T(256)}, f32[256]{0:T(256)S(1)}, u32[]{:S(2)}) copy-start(f32[256]{0:T(256)S(1)} %add_rsqrt_fusion.1) | copy-start | bytes 3076
  13.8 131.6 %all-gather.14.cloned.1.call-start = ((), (), s32[]{:S(2)}) async-start(), calls=%async_computation.10 | async-start | bytes 2621440 | tf_op jit(solution)/shard_map/all_gather | solution.py:117
  27.4 143.3 %all-gather.20.cloned.1.call-start = ((), (), s32[]{:S(2)}) async-start(), calls=%async_computation.13 | async-start | bytes 1511424 | tf_op jit(solution)/shard_map/all_gather | solution.py:122
  28.0 190.1 %all-gather.24.cloned.1.call-start = ((), (), s32[]{:S(2)}) async-start(), calls=%async_computation.18 | async-start | bytes 2621440 | tf_op jit(solution)/shard_map/all_gather | solution.py:127
  28.6 220.8 %all-gather.18.cloned.1.call-start = ((), (), s32[]{:S(2)}) async-start(), calls=%async_computation.12 | async-start | bytes 3022848 | tf_op jit(solution)/shard_map/all_gather | solution.py:121
  41.7 50.3 %copy-start.20 = (f32[1024,32]{0,1:T(8,128)}, f32[1024,32]{0,1:T(8,128)S(1)}, u32[]{:S(2)}) copy-start(f32[1024,32]{0,1:T(8,128)S(1)} %get-tuple-element.64) | copy-start | bytes 393220
  104.2 41.2 %copy-start.3 = (bf16[1,256,1024]{2,1,0:T(8,128)(2,1)S(1)}, bf16[1,256,1024]{2,1,0:T(8,128)(2,1)}, u32[]{:S(2)}) copy-start(bf16[1,256,1024]{2,1,0:T(8,128)(2,1)} %param.9) | copy-start | bytes 1572868
  104.3 41.1 %copy-start.14 = (bf16[1024,4,64]{0,2,1:T(8,128)(2,1)}, bf16[1024,4,64]{0,2,1:T(8,128)(2,1)S(1)}, u32[]{:S(2)}) copy-start(bf16[1024,4,64]{0,2,1:T(8,128)(2,1)S(1)} %maximum_convert_fusion) | copy-start | bytes 1572868
  105.6 39.8 %all-to-all-start = ((bf16[4,256,256]{1,2,0:T(8,128)(2,1)}), bf16[4,256,256]{1,2,0:T(8,128)(2,1)S(1)}, u32[]{:S(2)}, u32[]{:S(2)}) async-start(bf16[4,256,256]{1,2,0:T(8,128)(2,1)} %copy.33), calls=%async_computation | async-start | bytes 1048576 | tf_op jit(solution)/shard_map/all_to_all | solution.py:116
  109.0 39.1 %copy-start.25 = (f32[1024]{0:T(1024)S(1)}, f32[1024]{0:T(1024)}, u32[]{:S(2)}) copy-start(f32[1024]{0:T(1024)} %param.14) | copy-start | bytes 12292
  109.1 188.4 %all-gather.16.cloned.1.call-start = ((), (), s32[]{:S(2)}) async-start(), calls=%async_computation.11 | async-start | bytes 2621440 | tf_op jit(solution)/shard_map/all_gather | solution.py:126
  149.1 244.7 %reduce-scatter.18.cloned.1.call-start = ((), (), s32[]{:S(2)}) async-start(), calls=%async_computation.15 | async-start | bytes 5242880 | tf_op jit(solution)/shard_map/reduce_scatter | solution.py:160
  318.2 122.4 %reduce-scatter.16.cloned.1.call-start = ((), (), s32[]{:S(2)}) async-start(), calls=%async_computation.14 | async-start | bytes 2621440 | tf_op jit(solution)/shard_map/reduce_scatter | solution.py:131
  323.2 165.9 %all-gather.22.cloned.1.call-start = ((), (), s32[]{:S(2)}) async-start(), calls=%async_computation.16 | async-start | bytes 2621440 | tf_op jit(solution)/shard_map/all_gather | solution.py:168
  393.8 46.8 %copy-start.6 = (f32[256,1024]{1,0:T(8,128)S(1)}, f32[256,1024]{1,0:T(8,128)}, u32[]{:S(2)}) copy-start(f32[256,1024]{1,0:T(8,128)} %reduce-scatter.18.cloned.1.call-done) | copy-start | bytes 3145732
  443.7 98.8 %reduce-scatter.28.cloned.1.call-start = ((), (), s32[]{:S(2)}) async-start(), calls=%async_computation.22 | async-start | bytes 1769472
  461.9 115.9 %reduce-scatter.26.cloned.1.call-start = ((), (), s32[]{:S(2)}) async-start(), calls=%async_computation.21 | async-start | bytes 3244032
  485.1 130.3 %reduce-scatter.24.cloned.1.call-start = ((), (), s32[]{:S(2)}) async-start(), calls=%async_computation.20 | async-start | bytes 589824
  491.5 6.0 slice-start.3
  506.9 6.2 slice-start.1
  522.6 134.5 %reduce-scatter.22.cloned.1.call-start = ((), (), s32[]{:S(2)}) async-start(), calls=%async_computation.19 | async-start | bytes 1769472
  537.2 165.8 %reduce-scatter.20.cloned.1.call-start = ((), (), s32[]{:S(2)}) async-start(), calls=%async_computation.17 | async-start | bytes 2621440 | tf_op jit(solution)/shard_map/reduce_scatter | solution.py:214
  542.4 160.6 %copy-start.26 = (f32[1024]{0:T(1024)S(1)}, f32[1024]{0:T(1024)}, u32[]{:S(2)}) copy-start(f32[1024]{0:T(1024)} %param.11) | copy-start | bytes 12292
  542.4 160.6 %copy-start.36 = (f32[256]{0:T(256)S(1)}, f32[256]{0:T(256)}, u32[]{:S(2)}) copy-start(f32[256]{0:T(256)} %copy-done.35) | copy-start | bytes 3076
  542.4 160.6 %copy-start.39 = (f32[256]{0:T(256)S(1)}, f32[256]{0:T(256)}, u32[]{:S(2)}) copy-start(f32[256]{0:T(256)} %copy-done.38) | copy-start | bytes 3076
  544.3 160.3 %copy-start.37 = (f32[1024]{0:T(1024)S(1)}, f32[1024]{0:T(1024)}, u32[]{:S(2)}) copy-start(f32[1024]{0:T(1024)} %get-tuple-element.32) | copy-start | bytes 12292
  544.4 200.0 %copy-start.5 = (f32[256,1024]{1,0:T(8,128)S(1)}, f32[256,1024]{1,0:T(8,128)}, u32[]{:S(2)}) copy-start(f32[256,1024]{1,0:T(8,128)} %get-tuple-element.41) | copy-start | bytes 3145732
  (33 other events, 99.7 us)
Sparse Core Ops, SparseCore 0:
  10.5 29.3 all-gather.11
  42.0 45.9 all-gather.9
  89.6 55.7 all-gather.13
  147.1 23.5 all-gather.19
  172.1 45.9 all-gather.23
  219.8 29.4 all-gather.17
  251.5 45.9 all-gather.15
  318.3 75.4 reduce-scatter.17
  396.2 44.3 reduce-scatter.15
  443.8 45.2 all-gather.21
  492.4 37.2 reduce-scatter.27
  533.0 44.8 reduce-scatter.25
  581.2 34.1 reduce-scatter.23
  618.5 38.4 reduce-scatter.21
  659.2 43.8 reduce-scatter.19
where the time goes:
time: 764 us; the launch traced here: 754 us
  waiting for transfers between devices  497 us (65%)
  matrix products  81.8 us (11%)
  blocking collectives  64.4 us (8%)
  other arithmetic  41.2 us (5%)
  local copies, waits for them, and re-layouts  38.7 us (5%)
  starting transfers between devices  15.4 us (2%)
  between operations  15.1 us (2%)
    unnamed x19, waiting for transfers between devices  110 us
    reduce_scatter x1, waiting for transfers between devices, on_device(): lax.psum_scatter(jnp.einsum('clf,cdf->ld', grad_expanded, in_full, prefer...  70.6 us
    all_gather x1, waiting for transfers between devices, on_device(): lax.all_gather((scaled2 * norm2_gain).astype(jnp.bfloat16), 'tensor', axi...  48.1 us
    all_gather x1, waiting for transfers between devices, on_device(): lax.all_gather(out_grad[0], 'tensor', axis=0, tiled=True)  47.4 us
    all_gather x1, waiting for transfers between devices, on_device(): lax.all_gather((scaled1 * norm1_gain).astype(jnp.bfloat16), 'tensor', axi...  45.6 us
    reduce_scatter x1, waiting for transfers between devices, on_device(): lax.psum_scatter(jnp.einsum('cle,cde->ld', grad_projected, qkv_full, pref...  43.9 us
    reduce_scatter x1, waiting for transfers between devices, on_device(): lax.psum_scatter(jnp.dot(product, down_full, preferred_element_type=jnp.f...  43.9 us
    psum x1, blocking collectives, on_device(): lax.psum((gain1_term, gain2_term), ('dp', 'tensor'))  39.7 us
  transfers between devices with their start and end apart: 16, of which 13 were waited for; matrix products, arithmetic and copies ran while one was open for 17% of the time, Pallas kernels for 0%

commit v1 on v0

v1 whole, which is shorter than its diff:
```python
import functools

import jax
import jax.numpy as jnp
from jax import lax
from jax.experimental import pallas as pl
from jax.experimental.pallas import tpu as pltpu
from jax.sharding import PartitionSpec as P

HEAD_DIM = 64
HALF = HEAD_DIM // 2
EPSILON = 1e-05
ROPE_BASE = 160000.0
MASKED = -1e30
ROWS = 256
SCALE = HEAD_DIM ** (-0.5)
F32 = jnp.float32
BF16 = jnp.bfloat16


def dot(a, b, dims):
    return lax.dot_general(a, b, ((dims[0], dims[1]), ((), ())), preferred_element_type=F32)


NN = ((1,), (0,))
NT = ((1,), (1,))
TN = ((0,), (0,))


def spin(u, cosine, sine):
    width = u.shape[-1]
    lane = lax.broadcasted_iota(jnp.int32, u.shape, 1)
    other = jnp.where(
        lane % HEAD_DIM < HALF, pltpu.roll(u, width - HALF, 1), pltpu.roll(u, HALF, 1)
    )
    return u * cosine + other * sine


def head_mask(shape, head):
    lane = lax.broadcasted_iota(jnp.int32, shape, 1)
    return lane // HEAD_DIM == head


def attend_kernel(rows, normed, w_qkv, cosine, sine, seg_col, seg_row, q, k, v, ctx, lse):
    length, width = q.shape
    heads = width // HEAD_DIM

    @pl.loop(0, length // rows)
    def _(block):
        here = pl.ds(pl.multiple_of(block * rows, rows), rows)
        proj = dot(normed[here, :], w_qkv[...], NN)
        cos_here, sin_here = cosine[here, :], sine[here, :]
        q[here, :] = spin(proj[:, :width], cos_here, sin_here).astype(BF16)
        k[here, :] = spin(proj[:, width : 2 * width], cos_here, sin_here).astype(BF16)
        v[here, :] = proj[:, 2 * width :].astype(BF16)

    @pl.loop(0, length // rows)
    def _(block):
        here = pl.ds(pl.multiple_of(block * rows, rows), rows)
        q_here = q[here, :]
        same = seg_col[here, :] == seg_row[...]
        total = jnp.zeros((rows, width), F32)
        for head in range(heads):
            mine = head_mask((rows, width), head)
            q_head = jnp.where(mine, q_here, jnp.zeros_like(q_here)) * BF16(SCALE)
            scores = jnp.where(same, dot(q_head, k[...], NT), MASKED)
            highest = jnp.max(scores, axis=1, keepdims=True)
            weights = jnp.exp(scores - highest)
            sums = jnp.sum(weights, axis=1, keepdims=True)
            mixed = dot(weights.astype(BF16), v[...], NN) * (1.0 / sums)
            total = jnp.where(mine, mixed, total)
            lse[here, head : head + 1] = highest + jnp.log(sums)
        ctx[here, :] = total.astype(BF16)


def attend(normed, w_qkv, cosine, sine, seg_col, seg_row):
    length = normed.shape[0]
    width = w_qkv.shape[1] // 3
    rows = min(ROWS, length)
    heads = width // HEAD_DIM
    cost = pl.CostEstimate(
        flops=2 * length * normed.shape[1] * 3 * width + 4 * length * length * width * 4,
        bytes_accessed=8 * 2**20,
        transcendentals=heads * length * length,
    )
    wide = jax.ShapeDtypeStruct((length, width), BF16)
    return pl.pallas_call(
        functools.partial(attend_kernel, rows),
        out_shape=(wide, wide, wide, wide, jax.ShapeDtypeStruct((length, 128), F32)),
        compiler_params=pltpu.CompilerParams(vmem_limit_bytes=48 * 2**20),
        cost_estimate=cost,
        name="attend",
    )(normed, w_qkv, cosine, sine, seg_col, seg_row)


def attend_back_kernel(
    rows, dctx, q, k, v, lse_row, cosine, sine, seg_col, seg_row, dproj, dk_sum, dv_sum
):
    length, width = q.shape
    heads = width // HEAD_DIM
    dk_sum[...] = jnp.zeros_like(dk_sum)
    dv_sum[...] = jnp.zeros_like(dv_sum)

    @pl.loop(0, length // rows)
    def _(block):
        here = pl.ds(pl.multiple_of(block * rows, rows), rows)
        q_here, dctx_here = q[here, :], dctx[here, :]
        same = seg_col[...] == seg_row[:, here]
        dq = jnp.zeros((rows, width), F32)
        for head in range(heads):
            mine = head_mask((rows, width), head)
            q_head = jnp.where(mine, q_here, jnp.zeros_like(q_here)) * BF16(SCALE)
            dctx_head = jnp.where(mine, dctx_here, jnp.zeros_like(dctx_here))
            scores = jnp.where(same, dot(k[...], q_head, NT), MASKED)
            chances = jnp.exp(scores - lse_row[head : head + 1, here])
            grads = dot(v[...], dctx_head, NT)
            both = chances * grads
            inner = jnp.sum(both, axis=0, keepdims=True)
            dscores = (both - chances * inner).astype(BF16)
            dv_sum[...] += dot(chances.astype(BF16), dctx_head, NN)
            dk_sum[...] += dot(dscores, q_head, NN)
            dq = jnp.where(mine, dot(dscores, k[...], TN), dq)
        dq = spin(dq * SCALE, cosine[here, :], -sine[here, :])
        dproj[here, :width] = dq.astype(BF16)

    @pl.loop(0, length // rows)
    def _(block):
        here = pl.ds(pl.multiple_of(block * rows, rows), rows)
        dk = spin(dk_sum[here, :], cosine[here, :], -sine[here, :])
        dproj[here, width : 2 * width] = dk.astype(BF16)
        dproj[here, 2 * width :] = dv_sum[here, :].astype(BF16)


def attend_back(dctx, q, k, v, lse_row, cosine, sine, seg_col, seg_row):
    length, width = q.shape
    rows = min(ROWS, length)
    heads = width // HEAD_DIM
    cost = pl.CostEstimate(
        flops=10 * length * length * width * 4,
        bytes_accessed=8 * 2**20,
        transcendentals=heads * length * length,
    )
    return pl.pallas_call(
        functools.partial(attend_back_kernel, rows),
        out_shape=jax.ShapeDtypeStruct((length, 3 * width), BF16),
        scratch_shapes=[pltpu.VMEM((length, width), F32), pltpu.VMEM((length, width), F32)],
        compiler_params=pltpu.CompilerParams(vmem_limit_bytes=48 * 2**20),
        cost_estimate=cost,
        name="attend_back",
    )(dctx, q, k, v, lse_row, cosine, sine, seg_col, seg_row)


def normalize(rows):
    average = jnp.mean(rows, axis=-1, keepdims=True)
    centred = rows - average
    inv_std = lax.rsqrt(jnp.mean(centred * centred, axis=-1, keepdims=True) + EPSILON)
    return centred * inv_std, inv_std


def norm_back(grads, gain, scaled, inv_std):
    inner = grads * gain
    mean_grad = jnp.mean(inner, axis=-1, keepdims=True)
    mean_proj = jnp.mean(inner * scaled, axis=-1, keepdims=True)
    return inv_std * (inner - mean_grad - scaled * mean_proj)


def on_device(
    n_dp,
    n_t,
    block_in,
    segment_ids,
    norm1_gain,
    w_qkv,
    w_out,
    norm2_gain,
    w_in,
    w_mlp_out,
    out_grad,
):
    n_quad = n_dp // 2
    bits = [1 << b for b in range(n_quad.bit_length() - 1)]
    d_index, t_index = lax.axis_index("dp"), lax.axis_index("tensor")
    quad, first_core = d_index // 2, d_index % 2 == 0
    piece, d_model = block_in.shape[1], block_in.shape[2]
    length = piece * n_t
    width = w_qkv.shape[2]
    span = d_model // n_quad

    def core(x):
        return lax.ppermute(x, "dp", [(i, i ^ 1) for i in range(n_dp)])

    def pair(x, bit):
        return lax.ppermute(x, "dp", [(i, i ^ (2 * bit)) for i in range(n_dp)])

    def ahead(x, by):
        return lax.ppermute(x, "tensor", [(i, (i + by) % n_t) for i in range(n_t)])

    def across(x, mask):
        return lax.ppermute(x, "tensor", [(i, i ^ mask) for i in range(n_t)])

    def pick(a, b):
        return jnp.where(first_core, a, b)

    def reorder(x):
        cuts = [
            lax.dynamic_slice_in_dim(x, (quad ^ m) * span, span, axis=x.ndim - 1)
            for m in range(n_quad)
        ]
        return jnp.concatenate(cuts, axis=-1)

    def pair_gather(x, order):
        held = {0: x}
        for bit in order:
            held.update({m ^ bit: pair(block, bit) for m, block in list(held.items())})
        return [held[m] for m in range(n_quad)]

    def pair_scatter(blocks, order):
        held = dict(enumerate(blocks))
        for bit in order:
            held = {
                m: (held[m].astype(F32) + pair(held[m | bit], bit).astype(F32)).astype(BF16)
                for m in held
                if not m & bit
            }
        return held[0]

    def line_gather(x):
        return [x] + [ahead(x, -by) for by in range(1, n_t)]

    x = reorder(block_in[0]).astype(F32)
    gain1, gain2 = reorder(norm1_gain), reorder(norm2_gain)
    scaled1, inv_std1 = normalize(x)
    normed = jnp.concatenate(line_gather((scaled1 * gain1).astype(BF16)), axis=0)
    segments = jnp.concatenate(line_gather(segment_ids), axis=1)

    qkv_local = jnp.concatenate([w_qkv[0], w_qkv[1], w_qkv[2]], axis=1)
    qkv_mine = pair_gather(qkv_local, bits)
    qkv_other = [core(block) for block in qkv_mine]
    qkv_full = jnp.concatenate(
        [
            part
            for mine, other in zip(qkv_mine, qkv_other)
            for part in (pick(mine, other), pick(other, mine))
        ],
        axis=0,
    )
    out_mine = pair_gather(jnp.concatenate(line_gather(w_out), axis=0), bits)
    out_other = [core(block) for block in out_mine]
    out_full = jnp.concatenate(
        [
            part
            for mine, other in zip(out_mine, out_other)
            for part in (pick(mine, other), pick(other, mine))
        ],
        axis=1,
    )

    mlp_local = jnp.stack([w_in[0].T, w_in[1].T, w_mlp_out])
    slices = [mlp_local] + [across(mlp_local, mask) for mask in range(1, n_t)]
    chunks = []
    for j in range(n_t // 2):
        even, odd = slices[2 * j], slices[2 * j + 1]
        other = core(pick(odd, even))
        low = pair_gather(pick(even, other), bits[::-1])
        high = pair_gather(pick(other, odd), bits)
        chunks.append(
            jnp.concatenate([part for both in zip(low, high) for part in both], axis=-1)
        )

    places = (t_index * piece + jnp.arange(length, dtype=jnp.int32)) % length
    firsts = jnp.sum((segments < segments.reshape(length, 1)).astype(jnp.int32), axis=1)
    freqs = jnp.power(ROPE_BASE, -jnp.arange(HALF, dtype=F32) * 2.0 / HEAD_DIM)
    angles = (places - firsts).astype(F32)[:, None] * freqs[None, :]
    cosine, sine = jnp.cos(angles), jnp.sin(angles)
    cosine = jnp.tile(cosine, (1, width // HALF))
    sine = jnp.tile(jnp.concatenate([-sine, sine], axis=1), (1, width // HEAD_DIM))
    seg_col = segments.reshape(length, 1)
    q, k, v, ctx_local, lse = attend(normed, qkv_full, cosine, sine, seg_col, segments)
    lse_row = lse[:, : max(8, width // HEAD_DIM)].T

    ctx_pieces = [ctx_local[:piece]] + [
        ahead(ctx_local[s * piece : (s + 1) * piece], s) for s in range(1, n_t)
    ]
    ctx = jnp.concatenate([ctx_pieces[(n_t - s) % n_t] for s in range(n_t)], axis=1)
    hidden = x + dot(ctx, out_full, NN)

    scaled2, inv_std2 = normalize(hidden)
    normed2 = (scaled2 * gain2).astype(BF16)
    dy = reorder(out_grad[0])
    normed2_both = jnp.concatenate([normed2, core(normed2)], axis=0)
    dy_both = jnp.concatenate([dy, core(dy)], axis=0)
    mlp, dn2 = 0.0, 0.0
    mlp_grads = []
    for up, gate_up, down in chunks:
        act, gate = dot(normed2_both, up, NT), dot(normed2_both, gate_up, NT)
        dprod = dot(dy_both, down, NT)
        below = 0.5 * (1.0 + lax.erf(act * (0.5**0.5)))
        slope = below + act * jnp.exp(-0.5 * act * act) * 0.3989422804014327
        gelu = act * below
        prod = (gelu * gate).astype(BF16)
        dact = (dprod * gate * slope).astype(BF16)
        dgate = (dprod * gelu).astype(BF16)
        mlp += dot(prod, down, NN)
        dn2 += dot(dact, up, NN) + dot(dgate, gate_up, NN)
        mlp_grads.append(
            jnp.stack(
                [
                    dot(dact, normed2_both, TN).astype(BF16),
                    dot(dgate, normed2_both, TN).astype(BF16),
                    dot(prod, dy_both, TN).astype(BF16),
                ]
            )
        )
    mlp_own = mlp[:piece] + core(mlp[piece:].astype(BF16)).astype(F32)
    block_out = reorder((hidden + mlp_own).astype(BF16))
    dn2_own = dn2[:piece] + core(dn2[piece:].astype(BF16)).astype(F32)

    dh = dy.astype(F32) + norm_back(dn2_own, gain2, scaled2, inv_std2)
    gain2_part = jnp.sum(dn2_own * scaled2, axis=0)
    dh_low = dh.astype(BF16)

    dctx = dot(dh_low, out_full, NT).astype(BF16)
    dctx_pieces = [dctx[:, :width]] + [
        ahead(dctx[:, s * width : (s + 1) * width], s) for s in range(1, n_t)
    ]
    dctx_local = jnp.concatenate([dctx_pieces[(n_t - s) % n_t] for s in range(n_t)], axis=0)
    dproj = attend_back(dctx_local, q, k, v, lse_row, cosine, sine, seg_col, segments)
    dn1 = dot(dproj, qkv_full, NT)
    gain1_part = jnp.sum(dn1 * normed.astype(F32), axis=0) / gain1
    dn1_low = dn1.astype(BF16)
    dn1_own = dn1[:piece]
    for s in range(1, n_t):
        dn1_own = dn1_own + ahead(dn1_low[s * piece : (s + 1) * piece], s).astype(F32)
    in_grad = reorder(dh + norm_back(dn1_own, gain1, scaled1, inv_std1))

    block = d_model // n_dp
    ends = []
    for grads in mlp_grads:
        cuts = [grads[:, :, i * block : (i + 1) * block] for i in range(n_dp)]
        low = pair_scatter(cuts[0::2], bits)
        high = pair_scatter(cuts[1::2], bits[::-1])
        kept, other = pick(low, high), core(pick(high, low))
        ends += [pick(kept, other), pick(other, kept)]
    mlp_sum = ends[0].astype(F32)
    for mask in range(1, n_t):
        mlp_sum = mlp_sum + across(ends[mask], mask).astype(F32)
    w_in_grad = jnp.stack([mlp_sum[0].T, mlp_sum[1].T])

    def core_scatter(blocks):
        return [
            (pick(a, b).astype(F32) + core(pick(b, a)).astype(F32)).astype(BF16)
            for a, b in zip(blocks[0::2], blocks[1::2])
        ]

    out_partial = dot(ctx, dh_low, TN).astype(BF16)
    out_cuts = [out_partial[:, i * block : (i + 1) * block] for i in range(n_dp)]
    out_low = pair_scatter(core_scatter(out_cuts), bits)
    out_sum = out_low[:width].astype(F32)
    for s in range(1, n_t):
        out_sum = out_sum + ahead(out_low[s * width : (s + 1) * width], s).astype(F32)

    qkv_partial = dot(normed, dproj, TN).astype(BF16)
    qkv_cuts = [qkv_partial[i * block : (i + 1) * block] for i in range(n_dp)]
    qkv_sum = pair_scatter(core_scatter(qkv_cuts), bits).astype(F32)
    w_qkv_grad = jnp.stack([qkv_sum[:, c * width : (c + 1) * width] for c in range(3)])

    gains = reorder(jnp.stack([gain1_part, gain2_part]))
    gains = gains + core(gains)
    for bit in bits:
        gains = gains + pair(gains, bit)
    mask = 1
    while mask < n_t:
        gains = gains + across(gains, mask)
        mask *= 2
    return (
        block_out[None],
        in_grad[None],
        gains[0],
        w_qkv_grad,
        out_sum,
        gains[1],
        w_in_grad,
        mlp_sum[2],
    )


def solution(mesh):
    in_specs = (
        P("dp", "tensor", None),
        P("dp", "tensor"),
        P(),
        P(None, "dp", "tensor"),
        P("tensor", "dp"),
        P(),
        P(None, "dp", "tensor"),
        P("tensor", "dp"),
        P("dp", "tensor", None),
    )
    out_specs = (
        P("dp", "tensor", None),
        P("dp", "tensor", None),
        P(),
        P(None, "dp", "tensor"),
        P("tensor", "dp"),
        P(),
        P(None, "dp", "tensor"),
        P("tensor", "dp"),
    )
    return jax.shard_map(
        functools.partial(on_device, mesh.shape["dp"], mesh.shape["tensor"]),
        mesh=mesh,
        in_specs=in_specs,
        out_specs=out_specs,
        check_vma=False,
    )
```

time: 764 us -> 463 us (0.61)
  waiting for transfers between devices: 497 us -> 221 us
  starting transfers between devices: 15.4 us -> 110 us
  blocking collectives: 64.4 us -> 0 us
  matrix products: 81.8 us -> 28.9 us
  Pallas kernels: 0 us -> 33.2 us
  local copies, waits for them, and re-layouts: 38.7 us -> 23.7 us
  between operations: 15.1 us -> 2.86 us
    all_gather x8 -> x0, waiting for transfers between devices: 229 us -> none  [the longest x1 48.1 us: on_device(): lax.all_gather((scaled2 * norm2_gain).astype(jnp.bfloat16), 'tensor', axi...]
    ppermute x0 -> x92, waiting for transfers between devices: none -> 221 us  [the longest x38 111 us: pair(): return lax.ppermute(x, 'dp', [(i, i ^ 2 * bit) for i in range(n_dp)])]
    reduce_scatter x3 -> x0, waiting for transfers between devices: 158 us -> none  [the longest x1 70.6 us: on_device(): lax.psum_scatter(jnp.einsum('clf,cdf->ld', grad_expanded, in_full, prefer...]
    unnamed x19 -> x0, waiting for transfers between devices: 110 us -> none
    ppermute x0 -> x92, starting transfers between devices: none -> 110 us  [the longest x21 58.9 us: ahead(): return lax.ppermute(x, 'tensor', [(i, (i + by) % n_t) for i in range(n_t)])]
    dot_general x24 -> x23, matrix products: 81.8 us -> 28.9 us  [dot(): lax.dot_general(a, b, ((dims[0], dims[1]), ((), ())), preferred_element_t...]
    psum x1 -> x0, blocking collectives: 39.7 us -> none  [on_device(): lax.psum((gain1_term, gain2_term), ('dp', 'tensor'))]
    pallas_call x0 -> x2, Pallas kernels: none -> 33.2 us  [the longest x1 19.1 us: attend_back(): pl.pallas_call(functools.partial(attend_back_kernel, rows), out_shape=jax...]
  transfers between devices with their start and end apart: 16 -> 92, of which waited for: 13 -> 40; matrix products, arithmetic and copies ran while one was open for 17% -> 16% of each run, Pallas kernels for 0% -> 7%
where the time goes in v1:
time: 463 us; the launch traced here: 455 us
  waiting for transfers between devices  221 us (48%)
  starting transfers between devices  110 us (24%)
  other arithmetic  35.4 us (8%)
  Pallas kernels  33.2 us (7%)
  matrix products  28.9 us (6%)
  local copies, waits for them, and re-layouts  23.7 us (5%)
    ppermute x38, waiting for transfers between devices, pair(): return lax.ppermute(x, 'dp', [(i, i ^ 2 * bit) for i in range(n_dp)])  111 us
    ppermute x21, waiting for transfers between devices, ahead(): return lax.ppermute(x, 'tensor', [(i, (i + by) % n_t) for i in range(n_t)])  75.8 us
    ppermute x21, starting transfers between devices, ahead(): return lax.ppermute(x, 'tensor', [(i, (i + by) % n_t) for i in range(n_t)])  58.9 us
    ppermute x8, waiting for transfers between devices, across(): return lax.ppermute(x, 'tensor', [(i, i ^ mask) for i in range(n_t)])  33.5 us
    ppermute x38, starting transfers between devices, pair(): return lax.ppermute(x, 'dp', [(i, i ^ 2 * bit) for i in range(n_dp)])  32.7 us
    dot_general x23, matrix products, dot(): lax.dot_general(a, b, ((dims[0], dims[1]), ((), ())), preferred_element_t...  28.9 us
    pallas_call x1, Pallas kernels, attend_back(): pl.pallas_call(functools.partial(attend_back_kernel, rows), out_shape=jax...  19.1 us
    ppermute x8, starting transfers between devices, across(): return lax.ppermute(x, 'tensor', [(i, i ^ mask) for i in range(n_t)])  14.9 us
  transfers between devices with their start and end apart: 92, of which 40 were waited for; matrix products, arithmetic and copies ran while one was open for 16% of the time, Pallas kernels for 7%

profile of v1, /device:TPU:0, one launch (start us, length us, event | category | flops | bytes accessed | tf_op | source)
XLA Modules:
  0.0 455.1 jit_solution(1507180388804151699)
XLA Ops:
  0.7 5.1 %collective-permute-start.16 = (bf16[256,128]{1,0:T(8,128)(2,1)}, bf16[256,128]{1,0:T(8,128)(2,1)}, u32[]{:S(2)}, u32[]{:S(2)}) collective-permute-start(bf16[256,128]{1,0:T(8,128)(2,1)} %param.13), channel_id=1, source_target_pairs={{0,3},{1,0},{2,1},{3,2},{4,7},{5,4},{6,5},{7,6},{8,11},{9,8},{10,9... | collective-permute-start | bytes 196616 | tf_op jit(solution)/shard_map/ppermute | solution.py:196
  18.7 5.2 %collective-permute-done.12 = s32[1,256]{1,0:T(1,128)S(1)} collective-permute-done((s32[1,256]{1,0:T(1,128)S(1)}, s32[1,256]{1,0:T(1,128)S(1)}, u32[]{:S(2)}, u32[]{:S(2)}) %collective-permute-start.12) | collective-permute-done | bytes 1056 | tf_op jit(solution)/shard_map/ppermute | solution.py:196
  49.4 16.5 %collective-permute-done.35 = bf16[3,656,128]{2,1,0:T(8,128)(2,1)S(1)} collective-permute-done((bf16[3,656,128]{2,1,0:T(8,128)(2,1)}, bf16[3,656,128]{2,1,0:T(8,128)(2,1)S(1)}, u32[]{:S(2)}, u32[]{:S(2)}) %collective-permute-start.35) | collective-permute-done | bytes 503840 | tf_op jit(solution)/shard_map/ppermute | solution.py:199
  67.4 5.4 %collective-permute-done.8 = bf16[128,768]{1,0:T(8,128)(2,1)S(1)} collective-permute-done((bf16[128,768]{1,0:T(8,128)(2,1)}, bf16[128,768]{1,0:T(8,128)(2,1)S(1)}, u32[]{:S(2)}, u32[]{:S(2)}) %collective-permute-start.8) | collective-permute-done | bytes 196640 | tf_op jit(solution)/shard_map/ppermute | solution.py:193
  72.8 12.7 %collective-permute-done.27 = bf16[3,656,128]{2,1,0:T(8,128)(2,1)S(1)} collective-permute-done((bf16[3,656,128]{2,1,0:T(8,128)(2,1)S(1)}, bf16[3,656,128]{2,1,0:T(8,128)(2,1)S(1)}, u32[]{:S(2)}, u32[]{:S(2)}) %collective-permute-start.27) | collective-permute-done | bytes 503840 | tf_op jit(solution)/shard_map/ppermute | solution.py:199
  86.8 21.2 %collective-permute-done.1 = bf16[256,1024]{1,0:T(8,128)(2,1)S(1)} collective-permute-done((bf16[256,1024]{1,0:T(8,128)(2,1)S(1)}, bf16[256,1024]{1,0:T(8,128)(2,1)S(1)}, u32[]{:S(2)}, u32[]{:S(2)}) %collective-permute-start.1) | collective-permute-done | bytes 524320 | tf_op jit(solution)/shard_map/ppermute | solution.py:196
  113.8 14.0 %attend.1 = (bf16[1024,256]{1,0:T(8,128)(2,1)S(1)}, bf16[1024,256]{1,0:T(8,128)(2,1)S(1)}, bf16[1024,256]{1,0:T(8,128)(2,1)S(1)}, bf16[1024,256]{1,0:T(8,128)(2,1)S(1)}, f32[1024,128]{1,0:T(8,128)S(1)}) custom-call(bf16[1024,1024]{1,0:T(8,128)(2,1)} %pad_maximum_fusion.2.normed, bf16[1024,768]{1,0:T(8,128)(2,1)} %copy-done.59, f32[1024,256]{1,0:T(8,128)S(1)} %copy.31.cosine, ...), custom_call_target="tpu_custom_call" | custom-call | flops 5905580032 | bytes 8388608 | tf_op jit(solution)/shard_map/attend/pallas_call | solution.py:87
  129.8 11.3 %collective-permute-start.15 = (bf16[256,256]{1,0:T(8,128)(2,1)}, bf16[256,256]{1,0:T(8,128)(2,1)}, u32[]{:S(2)}, u32[]{:S(2)}) collective-permute-start(bf16[256,256]{1,0:T(8,128)(2,1)} %get-tuple-element.97), channel_id=1, source_target_pairs={{0,1},{1,2},{2,3},{3,0},{4,5},{5,6},{6,7},{7,4},{8,9},{9,10},{10,1... | collective-permute-start | bytes 393224 | tf_op jit(solution)/shard_map/ppermute | solution.py:196
  149.2 3.1 collective-permute-done.14
  164.6 6.8 %collective-permute-done.38 = bf16[3,656,128]{2,1,0:T(8,128)(2,1)S(1)} collective-permute-done((bf16[3,656,128]{2,1,0:T(8,128)(2,1)S(1)}, bf16[3,656,128]{2,1,0:T(8,128)(2,1)S(1)}, u32[]{:S(2)}, u32[]{:S(2)}) %collective-permute-start.38) | collective-permute-done | bytes 503840 | tf_op jit(solution)/shard_map/ppermute | solution.py:193
  172.1 10.1 %collective-permute-done.39 = bf16[3,656,128]{2,1,0:T(8,128)(2,1)S(1)} collective-permute-done((bf16[3,656,128]{2,1,0:T(8,128)(2,1)S(1)}, bf16[3,656,128]{2,1,0:T(8,128)(2,1)S(1)}, u32[]{:S(2)}, u32[]{:S(2)}) %collective-permute-start.39) | collective-permute-done | bytes 503840 | tf_op jit(solution)/shard_map/ppermute | solution.py:193
  185.4 7.6 %collective-permute-done.29 = bf16[3,656,128]{2,1,0:T(8,128)(2,1)S(1)} collective-permute-done((bf16[3,656,128]{2,1,0:T(8,128)(2,1)S(1)}, bf16[3,656,128]{2,1,0:T(8,128)(2,1)S(1)}, u32[]{:S(2)}, u32[]{:S(2)}) %collective-permute-start.29) | collective-permute-done | bytes 503840 | tf_op jit(solution)/shard_map/ppermute | solution.py:193
  193.6 10.1 %collective-permute-done.30 = bf16[3,656,128]{2,1,0:T(8,128)(2,1)S(1)} collective-permute-done((bf16[3,656,128]{2,1,0:T(8,128)(2,1)S(1)}, bf16[3,656,128]{2,1,0:T(8,128)(2,1)S(1)}, u32[]{:S(2)}, u32[]{:S(2)}) %collective-permute-start.30) | collective-permute-done | bytes 503840 | tf_op jit(solution)/shard_map/ppermute | solution.py:193
  208.1 6.5 %collective-permute-done.42 = bf16[3,656,128]{2,1,0:T(8,128)(2,1)S(1)} collective-permute-done((bf16[3,656,128]{2,1,0:T(8,128)(2,1)S(1)}, bf16[3,656,128]{2,1,0:T(8,128)(2,1)S(1)}, u32[]{:S(2)}, u32[]{:S(2)}) %collective-permute-start.42) | collective-permute-done | bytes 503840 | tf_op jit(solution)/shard_map/ppermute | solution.py:193
  219.3 5.3 %collective-permute-done.33 = bf16[3,656,128]{2,1,0:T(8,128)(2,1)S(1)} collective-permute-done((bf16[3,656,128]{2,1,0:T(8,128)(2,1)S(1)}, bf16[3,656,128]{2,1,0:T(8,128)(2,1)S(1)}, u32[]{:S(2)}, u32[]{:S(2)}) %collective-permute-start.33) | collective-permute-done | bytes 503840 | tf_op jit(solution)/shard_map/ppermute | solution.py:193
  248.4 4.9 %collective-permute-done.87 = bf16[3,656,128]{2,1,0:T(8,128)(2,1)S(1)} collective-permute-done((bf16[3,656,128]{2,1,0:T(8,128)(2,1)S(1)}, bf16[3,656,128]{2,1,0:T(8,128)(2,1)S(1)}, u32[]{:S(2)}, u32[]{:S(2)}) %collective-permute-start.87) | collective-permute-done | bytes 503840 | tf_op jit(solution)/shard_map/ppermute | solution.py:193
  255.7 8.0 %collective-permute-done.79 = bf16[3,656,128]{2,1,0:T(8,128)(2,1)S(1)} collective-permute-done((bf16[3,656,128]{2,1,0:T(8,128)(2,1)S(1)}, bf16[3,656,128]{2,1,0:T(8,128)(2,1)S(1)}, u32[]{:S(2)}, u32[]{:S(2)}) %collective-permute-start.79) | collective-permute-done | bytes 503840 | tf_op jit(solution)/shard_map/ppermute | solution.py:193
  268.7 4.1 collective-permute-start.49
  278.8 3.1 collective-permute-done.48
  282.1 19.1 %attend_back.1 = bf16[1024,768]{1,0:T(8,128)(2,1)} custom-call(bf16[1024,256]{1,0:T(8,128)(2,1)S(1)} %pad_maximum_fusion.9.dctx, bf16[1024,256]{1,0:T(8,128)(2,1)S(1)} %copy-done.1, bf16[1024,256]{1,0:T(8,128)(2,1)S(1)} %copy-done.3, bf16[1024,256]{1,0:T(8,128)(2,1)S(1)} %copy-done.5, f32[8,1024]{1,0:T(8,128)S(1)} %slice_bitcast_fusion.29.lse_row, ...), custom_call_target="tpu_custom_call" | custom-call | flops 10737418240 | bytes 8388608 | tf_op jit(solution)/shard_map/attend_back/pallas_call | solution.py:143
  301.3 3.8 multiply_reduce_fusion
  313.9 3.2 collective-permute-start.56
  329.9 7.2 %collective-permute-done.85 = bf16[3,656,128]{2,1,0:T(8,128)(2,1)S(1)} collective-permute-done((bf16[3,656,128]{2,1,0:T(8,128)(2,1)S(1)}, bf16[3,656,128]{2,1,0:T(8,128)(2,1)S(1)}, u32[]{:S(2)}, u32[]{:S(2)}) %collective-permute-start.85) | collective-permute-done | bytes 503840 | tf_op jit(solution)/shard_map/ppermute | solution.py:193
  339.6 8.3 %collective-permute-done.78 = bf16[3,656,128]{2,1,0:T(8,128)(2,1)S(1)} collective-permute-done((bf16[3,656,128]{2,1,0:T(8,128)(2,1)S(1)}, bf16[3,656,128]{2,1,0:T(8,128)(2,1)S(1)}, u32[]{:S(2)}, u32[]{:S(2)}) %collective-permute-start.78) | collective-permute-done | bytes 503840 | tf_op jit(solution)/shard_map/ppermute | solution.py:193
  351.2 3.7 collective-permute-done.77
  356.5 7.1 %collective-permute-done.70 = bf16[1024,128]{1,0:T(8,128)(2,1)S(1)} collective-permute-done((bf16[1024,128]{1,0:T(8,128)(2,1)S(1)}, bf16[1024,128]{1,0:T(8,128)(2,1)S(1)}, u32[]{:S(2)}, u32[]{:S(2)}) %collective-permute-start.70) | collective-permute-done | bytes 262176 | tf_op jit(solution)/shard_map/ppermute | solution.py:193
  364.5 5.7 %collective-permute-done.63 = bf16[128,768]{1,0:T(8,128)(2,1)S(1)} collective-permute-done((bf16[128,768]{1,0:T(8,128)(2,1)S(1)}, bf16[128,768]{1,0:T(8,128)(2,1)S(1)}, u32[]{:S(2)}, u32[]{:S(2)}) %collective-permute-start.63) | collective-permute-done | bytes 196640 | tf_op jit(solution)/shard_map/ppermute | solution.py:193
  371.2 18.2 %collective-permute-done.51 = bf16[256,1024]{1,0:T(8,128)(2,1)S(1)} collective-permute-done((bf16[256,1024]{1,0:T(8,128)(2,1)S(1)}, bf16[256,1024]{1,0:T(8,128)(2,1)S(1)}, u32[]{:S(2)}, u32[]{:S(2)}) %collective-permute-start.51) | collective-permute-done | bytes 524320 | tf_op jit(solution)/shard_map/ppermute | solution.py:196
  395.7 3.3 collective-permute-done.67
  399.4 5.9 %collective-permute-start.91 = (bf16[3,656,128]{2,1,0:T(8,128)(2,1)S(1)}, bf16[3,656,128]{2,1,0:T(8,128)(2,1)S(1)}, u32[]{:S(2)}, u32[]{:S(2)}) collective-permute-start(bf16[3,656,128]{2,1,0:T(8,128)(2,1)S(1)} %get-tuple-element.74), channel_id=1, source_target_pairs={{0,3},{1,2},{2,1},{3,0},{4,7},{5,6},{6,5},{7,4},{8,11},{9,10},{10,... | collective-permute-start | bytes 1511432 | tf_op jit(solution)/shard_map/ppermute | solution.py:199
  408.5 18.5 %collective-permute-start.72 = (bf16[256,128]{1,0:T(8,128)(2,1)S(1)}, bf16[256,128]{1,0:T(8,128)(2,1)S(1)}, u32[]{:S(2)}, u32[]{:S(2)}) collective-permute-start(bf16[256,128]{1,0:T(8,128)(2,1)S(1)} %get-tuple-element.109), channel_id=1, source_target_pairs={{0,1},{1,2},{2,3},{3,0},{4,5},{5,6},{6,7},{7,4},{8,9},{9,10},{10,1... | collective-permute-start | bytes 196616 | tf_op jit(solution)/shard_map/ppermute | solution.py:196
  427.8 24.1 %collective-permute-done.73 = bf16[256,128]{1,0:T(8,128)(2,1)S(1)} collective-permute-done((bf16[256,128]{1,0:T(8,128)(2,1)S(1)}, bf16[256,128]{1,0:T(8,128)(2,1)S(1)}, u32[]{:S(2)}, u32[]{:S(2)}) %collective-permute-start.73) | collective-permute-done | bytes 65568 | tf_op jit(solution)/shard_map/ppermute | solution.py:196
  (451 shorter events, 163.4 us)
Async XLA Ops:
  0.7 27.1 %collective-permute-start.16 = (bf16[256,128]{1,0:T(8,128)(2,1)}, bf16[256,128]{1,0:T(8,128)(2,1)}, u32[]{:S(2)}, u32[]{:S(2)}) collective-permute-start(bf16[256,128]{1,0:T(8,128)(2,1)} %param.13), channel_id=1, source_target_pairs={{0,3},{1,0},{2,1},{3,2},{4,7},{5,4},{6,5},{7,6},{8,11},{9,8},{10,9... | collective-permute-start | bytes 196616 | tf_op jit(solution)/shard_map/ppermute | solution.py:196
  5.8 25.1 %collective-permute-start.17 = (bf16[256,128]{1,0:T(8,128)(2,1)}, bf16[256,128]{1,0:T(8,128)(2,1)}, u32[]{:S(2)}, u32[]{:S(2)}) collective-permute-start(bf16[256,128]{1,0:T(8,128)(2,1)} %param.13), channel_id=1, source_target_pairs={{0,2},{1,3},{2,0},{3,1},{4,6},{5,7},{6,4},{7,5},{8,10},{9,11},{10,... | collective-permute-start | bytes 196616 | tf_op jit(solution)/shard_map/ppermute | solution.py:196
  5.8 26.7 %collective-permute-start.18 = (bf16[256,128]{1,0:T(8,128)(2,1)}, bf16[256,128]{1,0:T(8,128)(2,1)}, u32[]{:S(2)}, u32[]{:S(2)}) collective-permute-start(bf16[256,128]{1,0:T(8,128)(2,1)} %param.13), channel_id=1, source_target_pairs={{0,1},{1,2},{2,3},{3,0},{4,5},{5,6},{6,7},{7,4},{8,9},{9,10},{10,1... | collective-permute-start | bytes 196616 | tf_op jit(solution)/shard_map/ppermute | solution.py:196
  30.9 35.0 %collective-permute-start.35 = (bf16[3,656,128]{2,1,0:T(8,128)(2,1)}, bf16[3,656,128]{2,1,0:T(8,128)(2,1)S(1)}, u32[]{:S(2)}, u32[]{:S(2)}) collective-permute-start(bf16[3,656,128]{2,1,0:T(8,128)(2,1)} %pad_maximum_fusion.10), channel_id=1, source_target_pairs={{0,2},{1,3},{2,0},{3,1},{4,6},{5,7},{6,4},{7,5},{8,10},{9,11},{10,... | collective-permute-start | bytes 1511432 | tf_op jit(solution)/shard_map/ppermute | solution.py:199
  32.4 33.5 %collective-permute-start.36 = (bf16[3,656,128]{2,1,0:T(8,128)(2,1)}, bf16[3,656,128]{2,1,0:T(8,128)(2,1)S(1)}, u32[]{:S(2)}, u32[]{:S(2)}) collective-permute-start(bf16[3,656,128]{2,1,0:T(8,128)(2,1)} %pad_maximum_fusion.10), channel_id=1, source_target_pairs={{0,3},{1,2},{2,1},{3,0},{4,7},{5,6},{6,5},{7,4},{8,11},{9,10},{10,... | collective-permute-start | bytes 1511432 | tf_op jit(solution)/shard_map/ppermute | solution.py:199
  40.7 44.8 %collective-permute-start.27 = (bf16[3,656,128]{2,1,0:T(8,128)(2,1)S(1)}, bf16[3,656,128]{2,1,0:T(8,128)(2,1)S(1)}, u32[]{:S(2)}, u32[]{:S(2)}) collective-permute-start(bf16[3,656,128]{2,1,0:T(8,128)(2,1)S(1)} %copy-done.52), channel_id=1, source_target_pairs={{0,1},{1,0},{2,3},{3,2},{4,5},{5,4},{6,7},{7,6},{8,9},{9,8},{10,11... | collective-permute-start | bytes 1511432 | tf_op jit(solution)/shard_map/ppermute | solution.py:199
  45.6 41.2 %collective-permute-start.2 = (bf16[256,1024]{1,0:T(8,128)(2,1)S(1)}, bf16[256,1024]{1,0:T(8,128)(2,1)S(1)}, u32[]{:S(2)}, u32[]{:S(2)}) collective-permute-start(bf16[256,1024]{1,0:T(8,128)(2,1)S(1)} %copy-done.17), channel_id=1, source_target_pairs={{0,1},{1,2},{2,3},{3,0},{4,5},{5,6},{6,7},{7,4},{8,9},{9,10},{10,1... | collective-permute-start | bytes 1572872 | tf_op jit(solution)/shard_map/ppermute | solution.py:196
  48.4 59.6 %collective-permute-start.1 = (bf16[256,1024]{1,0:T(8,128)(2,1)S(1)}, bf16[256,1024]{1,0:T(8,128)(2,1)S(1)}, u32[]{:S(2)}, u32[]{:S(2)}) collective-permute-start(bf16[256,1024]{1,0:T(8,128)(2,1)S(1)} %copy-done.17), channel_id=1, source_target_pairs={{0,2},{1,3},{2,0},{3,1},{4,6},{5,7},{6,4},{7,5},{8,10},{9,11},{10,... | collective-permute-start | bytes 1572872 | tf_op jit(solution)/shard_map/ppermute | solution.py:196
  65.8 42.2 %collective-permute-start = (bf16[256,1024]{1,0:T(8,128)(2,1)S(1)}, bf16[256,1024]{1,0:T(8,128)(2,1)S(1)}, u32[]{:S(2)}, u32[]{:S(2)}) collective-permute-start(bf16[256,1024]{1,0:T(8,128)(2,1)S(1)} %copy-done.17), channel_id=1, source_target_pairs={{0,3},{1,0},{2,1},{3,2},{4,7},{5,4},{6,5},{7,6},{8,11},{9,8},{10,9... | collective-permute-start | bytes 1572872 | tf_op jit(solution)/shard_map/ppermute | solution.py:196
  72.8 37.3 %collective-permute-start.21 = (bf16[1024,128]{1,0:T(8,128)(2,1)S(1)}, bf16[1024,128]{1,0:T(8,128)(2,1)S(1)}, u32[]{:S(2)}, u32[]{:S(2)}) collective-permute-start(bf16[1024,128]{1,0:T(8,128)(2,1)S(1)} %collective-permute-done.20), channel_id=1, source_target_pairs={{0,4},{4,0},{8,12},{12,8},{16,20},{20,16},{24,28},{28,24},{1,5},{5... | collective-permute-start | bytes 786440 | tf_op jit(solution)/shard_map/ppermute | solution.py:190
  108.1 48.2 %collective-permute-start.37 = (bf16[3,656,128]{2,1,0:T(8,128)(2,1)}, bf16[3,656,128]{2,1,0:T(8,128)(2,1)}, u32[]{:S(2)}, u32[]{:S(2)}) collective-permute-start(bf16[3,656,128]{2,1,0:T(8,128)(2,1)} %broadcast_select_fusion.9), channel_id=1, source_target_pairs={{0,4},{4,0},{8,12},{12,8},{16,20},{20,16},{24,28},{28,24},{1,5},{5... | collective-permute-start | bytes 1511432 | tf_op jit(solution)/shard_map/ppermute | solution.py:190
  110.1 52.3 %collective-permute-start.28 = (bf16[3,656,128]{2,1,0:T(8,128)(2,1)}, bf16[3,656,128]{2,1,0:T(8,128)(2,1)}, u32[]{:S(2)}, u32[]{:S(2)}) collective-permute-start(bf16[3,656,128]{2,1,0:T(8,128)(2,1)} %broadcast_select_fusion.12), channel_id=1, source_target_pairs={{0,4},{4,0},{8,12},{12,8},{16,20},{20,16},{24,28},{28,24},{1,5},{5... | collective-permute-start | bytes 1511432 | tf_op jit(solution)/shard_map/ppermute | solution.py:190
  110.2 34.7 %collective-permute-start.25 = (bf16[1024,128]{1,0:T(8,128)(2,1)}, bf16[1024,128]{1,0:T(8,128)(2,1)}, u32[]{:S(2)}, u32[]{:S(2)}) collective-permute-start(bf16[1024,128]{1,0:T(8,128)(2,1)} %collective-permute-done.24), channel_id=1, source_target_pairs={{0,4},{4,0},{8,12},{12,8},{16,20},{20,16},{24,28},{28,24},{1,5},{5... | collective-permute-start | bytes 786440 | tf_op jit(solution)/shard_map/ppermute | solution.py:190
  157.6 25.3 %collective-permute-start.40 = (bf16[3,656,128]{2,1,0:T(8,128)(2,1)S(1)}, bf16[3,656,128]{2,1,0:T(8,128)(2,1)S(1)}, u32[]{:S(2)}, u32[]{:S(2)}) collective-permute-start(bf16[3,656,128]{2,1,0:T(8,128)(2,1)S(1)} %get-tuple-element.37), channel_id=1, source_target_pairs={{0,16},{4,20},{8,24},{12,28},{16,0},{20,4},{24,8},{28,12},{1,17},{... | collective-permute-start | bytes 1511432 | tf_op jit(solution)/shard_map/ppermute | solution.py:193
  162.6 30.3 %collective-permute-start.29 = (bf16[3,656,128]{2,1,0:T(8,128)(2,1)S(1)}, bf16[3,656,128]{2,1,0:T(8,128)(2,1)S(1)}, u32[]{:S(2)}, u32[]{:S(2)}) collective-permute-start(bf16[3,656,128]{2,1,0:T(8,128)(2,1)S(1)} %get-tuple-element.33), channel_id=1, source_target_pairs={{0,8},{4,12},{8,0},{12,4},{16,24},{20,28},{24,16},{28,20},{1,9},{5... | collective-permute-start | bytes 1511432 | tf_op jit(solution)/shard_map/ppermute | solution.py:193
  171.4 32.4 %collective-permute-start.30 = (bf16[3,656,128]{2,1,0:T(8,128)(2,1)S(1)}, bf16[3,656,128]{2,1,0:T(8,128)(2,1)S(1)}, u32[]{:S(2)}, u32[]{:S(2)}) collective-permute-start(bf16[3,656,128]{2,1,0:T(8,128)(2,1)S(1)} %get-tuple-element.31), channel_id=1, source_target_pairs={{0,8},{4,12},{8,0},{12,4},{16,24},{20,28},{24,16},{28,20},{1,9},{5... | collective-permute-start | bytes 1511432 | tf_op jit(solution)/shard_map/ppermute | solution.py:193
  184.6 29.9 %collective-permute-start.42 = (bf16[3,656,128]{2,1,0:T(8,128)(2,1)S(1)}, bf16[3,656,128]{2,1,0:T(8,128)(2,1)S(1)}, u32[]{:S(2)}, u32[]{:S(2)}) collective-permute-start(bf16[3,656,128]{2,1,0:T(8,128)(2,1)S(1)} %collective-permute-done.40), channel_id=1, source_target_pairs={{0,8},{4,12},{8,0},{12,4},{16,24},{20,28},{24,16},{28,20},{1,9},{5... | collective-permute-start | bytes 1511432 | tf_op jit(solution)/shard_map/ppermute | solution.py:193
  233.3 32.5 %collective-permute-start.46 = (bf16[256,1024]{1,0:T(8,128)(2,1)S(1)}, bf16[256,1024]{1,0:T(8,128)(2,1)S(1)}, u32[]{:S(2)}, u32[]{:S(2)}) collective-permute-start(bf16[256,1024]{1,0:T(8,128)(2,1)S(1)} %slice.399), channel_id=1, source_target_pairs={{0,4},{4,0},{8,12},{12,8},{16,20},{20,16},{24,28},{28,24},{1,5},{5... | collective-permute-start | bytes 1572872 | tf_op jit(solution)/shard_map/ppermute | solution.py:190
  253.9 71.0 %collective-permute-start.83 = (bf16[3,656,128]{2,1,0:T(8,128)(2,1)}, bf16[3,656,128]{2,1,0:T(8,128)(2,1)}, u32[]{:S(2)}, u32[]{:S(2)}) collective-permute-start(bf16[3,656,128]{2,1,0:T(8,128)(2,1)} %get-tuple-element.49), channel_id=1, source_target_pairs={{0,8},{4,12},{8,0},{12,4},{16,24},{20,28},{24,16},{28,20},{1,9},{5... | collective-permute-start | bytes 1511432 | tf_op jit(solution)/shard_map/ppermute | solution.py:193
  263.7 62.5 %collective-permute-start.86 = (bf16[3,656,128]{2,1,0:T(8,128)(2,1)}, bf16[3,656,128]{2,1,0:T(8,128)(2,1)}, u32[]{:S(2)}, u32[]{:S(2)}) collective-permute-start(bf16[3,656,128]{2,1,0:T(8,128)(2,1)} %get-tuple-element.46), channel_id=1, source_target_pairs={{0,16},{4,20},{8,24},{12,28},{16,0},{20,4},{24,8},{28,12},{1,17},{... | collective-permute-start | bytes 1511432 | tf_op jit(solution)/shard_map/ppermute | solution.py:193
  278.3 48.5 %collective-permute-start.75 = (bf16[3,656,128]{2,1,0:T(8,128)(2,1)}, bf16[3,656,128]{2,1,0:T(8,128)(2,1)S(1)}, u32[]{:S(2)}, u32[]{:S(2)}) collective-permute-start(bf16[3,656,128]{2,1,0:T(8,128)(2,1)} %get-tuple-element.43), channel_id=1, source_target_pairs={{0,8},{4,12},{8,0},{12,4},{16,24},{20,28},{24,16},{28,20},{1,9},{5... | collective-permute-start | bytes 1511432 | tf_op jit(solution)/shard_map/ppermute | solution.py:193
  326.8 28.1 %collective-permute-start.77 = (bf16[3,656,128]{2,1,0:T(8,128)(2,1)S(1)}, bf16[3,656,128]{2,1,0:T(8,128)(2,1)S(1)}, u32[]{:S(2)}, u32[]{:S(2)}) collective-permute-start(bf16[3,656,128]{2,1,0:T(8,128)(2,1)S(1)} %copy-done.49), channel_id=1, source_target_pairs={{0,16},{4,20},{8,24},{12,28},{16,0},{20,4},{24,8},{28,12},{1,17},{... | collective-permute-start | bytes 1511432 | tf_op jit(solution)/shard_map/ppermute | solution.py:193
  328.3 26.5 %collective-permute-start.80 = (bf16[3,656,128]{2,1,0:T(8,128)(2,1)S(1)}, bf16[3,656,128]{2,1,0:T(8,128)(2,1)S(1)}, u32[]{:S(2)}, u32[]{:S(2)}) collective-permute-start(bf16[3,656,128]{2,1,0:T(8,128)(2,1)S(1)} %get-tuple-element.44), channel_id=1, source_target_pairs={{0,8},{4,12},{8,0},{12,4},{16,24},{20,28},{24,16},{28,20},{1,9},{5... | collective-permute-start | bytes 1511432 | tf_op jit(solution)/shard_map/ppermute | solution.py:193
  350.4 38.9 %collective-permute-start.51 = (bf16[256,1024]{1,0:T(8,128)(2,1)S(1)}, bf16[256,1024]{1,0:T(8,128)(2,1)S(1)}, u32[]{:S(2)}, u32[]{:S(2)}) collective-permute-start(bf16[256,1024]{1,0:T(8,128)(2,1)S(1)} %get-tuple-element.66), channel_id=1, source_target_pairs={{0,2},{1,3},{2,0},{3,1},{4,6},{5,7},{6,4},{7,5},{8,10},{9,11},{10,... | collective-permute-start | bytes 1572872 | tf_op jit(solution)/shard_map/ppermute | solution.py:196
  350.8 39.1 %collective-permute-start.50 = (bf16[256,1024]{1,0:T(8,128)(2,1)S(1)}, bf16[256,1024]{1,0:T(8,128)(2,1)S(1)}, u32[]{:S(2)}, u32[]{:S(2)}) collective-permute-start(bf16[256,1024]{1,0:T(8,128)(2,1)S(1)} %get-tuple-element.64), channel_id=1, source_target_pairs={{0,1},{1,2},{2,3},{3,0},{4,5},{5,6},{6,7},{7,4},{8,9},{9,10},{10,1... | collective-permute-start | bytes 1572872 | tf_op jit(solution)/shard_map/ppermute | solution.py:196
  364.4 31.3 %collective-permute-start.65 = (bf16[1024,128]{1,0:T(8,128)(2,1)S(1)}, bf16[1024,128]{1,0:T(8,128)(2,1)S(1)}, u32[]{:S(2)}, u32[]{:S(2)}) collective-permute-start(bf16[1024,128]{1,0:T(8,128)(2,1)S(1)} %copy-done.54), channel_id=1, source_target_pairs={{0,4},{4,0},{8,12},{12,8},{16,20},{20,16},{24,28},{28,24},{1,5},{5... | collective-permute-start | bytes 786440 | tf_op jit(solution)/shard_map/ppermute | solution.py:190
  370.3 25.4 %collective-permute-start.71 = (bf16[1024,128]{1,0:T(8,128)(2,1)S(1)}, bf16[1024,128]{1,0:T(8,128)(2,1)S(1)}, u32[]{:S(2)}, u32[]{:S(2)}) collective-permute-start(bf16[1024,128]{1,0:T(8,128)(2,1)S(1)} %get-tuple-element.63), channel_id=1, source_target_pairs={{0,16},{4,20},{8,24},{12,28},{16,0},{20,4},{24,8},{28,12},{1,17},{... | collective-permute-start | bytes 786440 | tf_op jit(solution)/shard_map/ppermute | solution.py:193
  399.4 53.2 %collective-permute-start.91 = (bf16[3,656,128]{2,1,0:T(8,128)(2,1)S(1)}, bf16[3,656,128]{2,1,0:T(8,128)(2,1)S(1)}, u32[]{:S(2)}, u32[]{:S(2)}) collective-permute-start(bf16[3,656,128]{2,1,0:T(8,128)(2,1)S(1)} %get-tuple-element.74), channel_id=1, source_target_pairs={{0,3},{1,2},{2,1},{3,0},{4,7},{5,6},{6,5},{7,4},{8,11},{9,10},{10,... | collective-permute-start | bytes 1511432 | tf_op jit(solution)/shard_map/ppermute | solution.py:199
  405.3 47.3 %collective-permute-start.90 = (bf16[3,656,128]{2,1,0:T(8,128)(2,1)S(1)}, bf16[3,656,128]{2,1,0:T(8,128)(2,1)S(1)}, u32[]{:S(2)}, u32[]{:S(2)}) collective-permute-start(bf16[3,656,128]{2,1,0:T(8,128)(2,1)S(1)} %get-tuple-element.73), channel_id=1, source_target_pairs={{0,2},{1,3},{2,0},{3,1},{4,6},{5,7},{6,4},{7,5},{8,10},{9,11},{10,... | collective-permute-start | bytes 1511432 | tf_op jit(solution)/shard_map/ppermute | solution.py:199
  405.4 47.2 %collective-permute-start.82 = (bf16[3,656,128]{2,1,0:T(8,128)(2,1)S(1)}, bf16[3,656,128]{2,1,0:T(8,128)(2,1)S(1)}, u32[]{:S(2)}, u32[]{:S(2)}) collective-permute-start(bf16[3,656,128]{2,1,0:T(8,128)(2,1)S(1)} %broadcast_select_fusion.4), channel_id=1, source_target_pairs={{0,1},{1,0},{2,3},{3,2},{4,5},{5,4},{6,7},{7,6},{8,9},{9,8},{10,11... | collective-permute-start | bytes 1511432 | tf_op jit(solution)/shard_map/ppermute | solution.py:199
  406.1 45.7 %collective-permute-start.73 = (bf16[256,128]{1,0:T(8,128)(2,1)S(1)}, bf16[256,128]{1,0:T(8,128)(2,1)S(1)}, u32[]{:S(2)}, u32[]{:S(2)}) collective-permute-start(bf16[256,128]{1,0:T(8,128)(2,1)S(1)} %get-tuple-element.111), channel_id=1, source_target_pairs={{0,2},{1,3},{2,0},{3,1},{4,6},{5,7},{6,4},{7,5},{8,10},{9,11},{10,... | collective-permute-start | bytes 196616 | tf_op jit(solution)/shard_map/ppermute | solution.py:196
  408.5 43.3 %collective-permute-start.72 = (bf16[256,128]{1,0:T(8,128)(2,1)S(1)}, bf16[256,128]{1,0:T(8,128)(2,1)S(1)}, u32[]{:S(2)}, u32[]{:S(2)}) collective-permute-start(bf16[256,128]{1,0:T(8,128)(2,1)S(1)} %get-tuple-element.109), channel_id=1, source_target_pairs={{0,1},{1,2},{2,3},{3,0},{4,5},{5,6},{6,7},{7,4},{8,9},{9,10},{10,1... | collective-permute-start | bytes 196616 | tf_op jit(solution)/shard_map/ppermute | solution.py:196
  (134 other events, 1539.4 us)
